TPU v7x, 128 devices: a whole 4x4x4 slice. The times are simulated.
128 devices in a mesh: seg: 16 (over y, x), head: 8 (over z, core).
Axes of the slice: x: 4, y: 4, z: 4, core: 2. Of those that a mesh axis runs over, the one named last changes fastest.
Arguments:
- queries: bfloat16 [128, 256, 5120], P(('seg', 'head')), may hold values from -6 to 6
- key_states: bfloat16 [128, 256, 1024], P(('seg', 'head')), may hold values from -6 to 6
- values: bfloat16 [128, 256, 1024], P(('seg', 'head')), may hold values from -6 to 6
- grad_out: bfloat16 [128, 256, 5120], P(('seg', 'head')), may hold values from -6 to 6
- owners: int32 [128], replicated, may hold values from 0 to 127, as said below
- parents: int32 [128], replicated, may hold values from -1 to 31, as said below
- depths: int32 [128], replicated, may hold values from 0 to 2, as said below
- lengths: int32 [128], replicated, may hold values from 64 to 256, as said below
Outputs:
- query_grads: bfloat16 [128, 256, 5120], P(('seg', 'head'))
- key_grads: bfloat16 [128, 256, 1024], P(('seg', 'head'))
- value_grads: bfloat16 [128, 256, 1024], P(('seg', 'head'))
Inputs may be any that keep to these rules, and one draw needn't show every extreme that they name: A permutation: segment g sits in slot owners[g], on the index owners[g] // 8 of seg; each index of seg holds exactly 2 segments that have children. -1 exactly for the 8 roots, segments 0 to 7; any other segment's parent has a smaller number; segments 8 to 31 have roots as parents; every segment below 32 has a child and none from 32 on. `depths`: the number of ancestors: 0 for roots, else one more than the parent's. The first lengths[g] positions of a segment's slot are tokens, the rest padding.
All inputs are finite; a program needn't handle non-finite values.
Results may differ from a plain program's by a relative error of at most 0.014.
Values may be sent and summed in bfloat16 or wider, within the bound.
A program may use at most 128 MiB of HBM per device.

v0:
```python
import jax
import jax.numpy as jnp
from jax import lax
from jax.experimental import pallas as pl
from jax.experimental.pallas import tpu as pltpu
from jax.sharding import PartitionSpec as P

DH = 128
PUB = 2
MESH = pl.DeviceIdType.MESH
SIDE = 4
NHEAD = 8
NCOL = 16
BF = jnp.bfloat16
F32 = jnp.float32
NEG = -1e30

T_PUB, T_ANC, T_ORDER, T_CONT, T_LAST, T_RANK, T_OWN = 0, 2, 18, 34, 50, 83, 91
T_SIZE = 96


def table_kernel(owners, parents, depths, lengths, out, inverse, shared):
    col = lax.axis_index("seg")
    mine = lax.axis_index("head")
    count = owners.shape[0]

    for g in range(count):
        inverse[owners[g]] = g
    for slot in range(count):
        if slot % NHEAD == 0:
            rank = 0
        g = inverse[slot]
        inner = g < NCOL * PUB
        place = (slot // NHEAD) * PUB + rank

        @pl.when(inner)
        def _():
            shared[g] = place

        rank = rank + inner.astype(jnp.int32)
    targets = []
    rank = 0
    for p in range(NHEAD):
        g = inverse[col * NHEAD + p]
        inner = g < NCOL * PUB
        out[T_RANK + p] = jnp.where(inner, rank, 0)

        @pl.when(inner)
        def _():
            out[T_PUB + rank] = p

        rank = rank + inner.astype(jnp.int32)
        up = parents[g]
        depth = depths[g]
        one = (depth >= 1) & (up >= 0)
        up = jnp.maximum(up, 0)
        up2 = parents[up]
        two = (depth >= 2) & one & (up2 >= 0)
        up2 = jnp.maximum(up2, 0)
        first = shared[up]
        second = shared[up2]
        out[T_ANC + 2 * p] = jnp.where(one, first, 0)
        out[T_ANC + 2 * p + 1] = jnp.where(two, second, 0)
        targets.append(jnp.where(one, first, NCOL * PUB))
        targets.append(jnp.where(two, second, NCOL * PUB))

        @pl.when(p == mine)
        def _():
            out[T_OWN] = lengths[g]
            out[T_OWN + 1] = jnp.where(one, lengths[up], 0)
            out[T_OWN + 2] = jnp.where(two, lengths[up2], 0)
            out[T_OWN + 3] = inner.astype(jnp.int32)

    n = len(targets)
    places = [0] * n
    again = [False] * n
    for b in range(n):
        for a in range(b):
            c = targets[a] <= targets[b]
            places[b] = places[b] + c.astype(jnp.int32)
            places[a] = places[a] + 1 - c.astype(jnp.int32)
            again[b] = again[b] | (targets[a] == targets[b])
    for j in range(NCOL * PUB + 1):
        out[T_LAST + j] = n
    for l in range(n):
        out[T_ORDER + places[l]] = l
        out[T_CONT + places[l]] = jnp.int32(0) + again[l]
        out[T_LAST + targets[l]] = places[l]


def tables_of(owners, parents, depths, lengths):
    smem = pl.BlockSpec(memory_space=pltpu.SMEM)
    return pl.pallas_call(
        table_kernel,
        out_shape=jax.ShapeDtypeStruct((T_SIZE,), jnp.int32),
        in_specs=[smem] * 4,
        out_specs=smem,
        scratch_shapes=[pltpu.SMEM((128,), jnp.int32), pltpu.SMEM((32,), jnp.int32)],
    )(owners, parents, depths, lengths)


PEERS = [(0, 1), (1, 0), (1, 1), (3, 0), (3, 1), (2, 0), (2, 1)]


def kernel(tab, q_ref, k_ref, v_ref, g_ref, dq_ref, dk_ref, dv_ref,
           qv, gv, kown, vown, all_k, all_v, sh_k, sh_v, sel_k, sel_v, anc_k, anc_v,
           own_k, own_v, fb_k, fb_v, far_k, far_v, accs_k, accs_v,
           half_k, half_v, full_k, full_v, fin_k, fin_v, ret_k, ret_v,
           dqv, bias, live, kc, vc, kt, ec, dcat, gs, qs, invs,
           send_sem, recv_sem, local_sem, out_sem):
    seg = lax.axis_index("seg")
    head = lax.axis_index("head")
    slot = qv.shape[0]
    mid = slot // 2
    y, x = seg // SIDE, seg % SIDE
    z, core = head // 2, head % 2

    def peer(step):
        dz, dc = step
        return ((z + dz) % SIDE) * 2 + (core + dc) % 2

    def along(axis, step):
        if axis == 0:
            return y * SIDE + (x + step) % SIDE
        return ((y + step) % SIDE) * SIDE + x

    def at(axis, da, db):
        if axis == 0:
            return ((y + db) % SIDE) * SIDE + (x + da) % SIDE
        return ((y + da) % SIDE) * SIDE + (x + db) % SIDE

    ids = [0]
    sent = []

    class Handle:
        def __init__(self, n, like, owner=None):
            self.n, self.like, self.owner = n, like, owner

        def copy(self):
            return pltpu.make_async_remote_copy(
                src_ref=self.like, dst_ref=self.like, send_sem=send_sem.at[self.n], recv_sem=recv_sem.at[self.n],
                device_id=(seg, head), device_id_type=MESH)

        def wait_recv(self):
            self.copy().wait_recv()

        def wait_send(self):
            self.copy().wait_send()

    one_block, half_block, two_blocks = sel_k.at[0], sel_k.at[0, pl.ds(0, mid)], sel_k.at[pl.ds(0, 2)]

    def reserve(count, like):
        handles = [Handle(ids[0] + n, like) for n in range(count)]
        ids[0] += count
        sent.extend(handles)
        return handles

    def start(n, src, dst, to_seg, to_head):
        pltpu.make_async_remote_copy(
            src_ref=src, dst_ref=dst, send_sem=send_sem.at[n], recv_sem=recv_sem.at[n],
            device_id=(to_seg, to_head), device_id_type=MESH).start()

    def push(src, dst, to_seg, to_head, like, owner=None):
        handle = Handle(ids[0], like, owner)
        ids[0] += 1
        sent.append(handle)
        start(handle.n, src, dst, to_seg, to_head)
        return handle

    def settle(buffer):
        for handle in [handle for handle in sent if handle.owner is buffer]:
            handle.wait_send()
            sent.remove(handle)

    barrier = pltpu.get_barrier_semaphore()
    for step in PEERS:
        pl.semaphore_signal(barrier, inc=1, device_id=(seg, peer(step)), device_id_type=MESH)
    for axis in (0, 1):
        for step in (1, 2, 3):
            pl.semaphore_signal(barrier, inc=1, device_id=(along(axis, step), head), device_id_type=MESH)
    pl.semaphore_wait(barrier, len(PEERS) + 6)

    def lanes(p):
        return pl.ds(pl.multiple_of(p * DH, DH), DH)

    def offer(src, dst):
        return [push(src.at[0, :, lanes(peer(step))], dst.at[head], seg, peer(step), one_block) for step in PEERS]

    first_k = offer(k_ref, all_k)
    loads = [
        pltpu.make_async_copy(src.at[0], dst, local_sem.at[n])
        for n, (src, dst) in enumerate(((k_ref, kown), (v_ref, vown), (q_ref, qv), (g_ref, gv)))
    ]
    for load in loads:
        load.start()

    length = tab[T_OWN]
    rows = lax.broadcasted_iota(jnp.int32, (slot, slot), 0)
    cols = lax.broadcasted_iota(jnp.int32, (slot, slot), 1)
    bias[0:slot, :] = jnp.where((rows <= cols) & (rows < length), 0.0, NEG)
    bias[slot:2 * slot, :] = jnp.where(rows < tab[T_OWN + 1], 0.0, NEG)
    bias[2 * slot:3 * slot, :] = jnp.where(rows < tab[T_OWN + 2], 0.0, NEG)
    row = lax.broadcasted_iota(jnp.int32, (slot, DH), 0)
    live[...] = jnp.where(row < length, 1.0, 0.0).astype(BF)

    class Gather:
        def __init__(self, sh, whole, own):
            self.sh, self.whole, self.own = sh, whole, own

        def block(self, r, da, db, part=None):
            ref = self.sh.at[at(r, da, db) * PUB + r]
            if part is None:
                return ref
            return ref.at[pl.ds(part * mid, mid)]

        def spread(self, r, axis, da, db):
            ref = self.block(r, da, db)
            return [push(ref, ref, along(axis, step), head, one_block, self.sh) for step in (1, 3)]

        def relay(self, r, axis, da, db, pair):
            out = []
            for part, copy in enumerate(pair):
                copy.wait_recv()
                step = 3 if part == 0 else 1
                ref = self.block(r, step if axis == r else da, db if axis == r else step, part)
                out.append(push(ref, ref, along(axis, 1 if part == 0 else 3), head,
                                half_block, self.sh))
            return out

        def steps(self):
            self.whole[head] = self.own[:, lanes(head)]
            for r in range(PUB):
                self.sh[seg * PUB + r] = self.whole[tab[T_PUB + r]]
            a, b, relays = {}, {}, []
            for r in range(PUB):
                ref = self.block(r, 0, 0)
                a[r] = [push(ref, ref, along(r, step), head, one_block, self.sh) for step in (1, 3, 2)]
            yield
            for r in range(PUB):
                b[r, 0] = self.spread(r, 1 - r, 0, 0)
            for r in range(PUB):
                for came, da in ((0, 3), (1, 1)):
                    a[r][came].wait_recv()
                    b[r, da] = self.spread(r, 1 - r, da, 0)
            yield
            for r in range(PUB):
                relays += self.relay(r, 1 - r, 0, 0, b[r, 0])
            for r in range(PUB):
                a[r][2].wait_recv()
                b[r, 2] = self.spread(r, 1 - r, 2, 0)
            yield
            for da in (3, 1):
                for r in range(PUB):
                    relays += self.relay(r, 1 - r, da, 0, b[r, da])
            yield
            for r in range(PUB):
                relays += self.relay(r, 1 - r, 2, 0, b[r, 2])
            yield
            for copy in relays:
                copy.wait_recv()

    def run(seq):
        for _ in seq:
            return True
        return False

    def select(sh, sel, anc):
        out = []
        for step in PEERS:
            p = peer(step)
            for a in range(2):
                sel[p * 2 + a] = sh[tab[T_ANC + 2 * p + a]]
            out.append(push(sel.at[pl.ds(p * 2, 2)], anc.at[pl.ds(head * 2, 2)], seg, p, two_blocks, sel))
        for a in range(2):
            anc[head * 2 + a] = sh[tab[T_ANC + 2 * head + a]]
        return out

    group = qv.shape[1] // kown.shape[1]
    scale = DH ** -0.5
    exp_scale = scale * 1.4426950408889634
    nt = (((1,), (1,)), ((), ()))

    def giver(n):
        m = n // 2
        dz = m + m // 2 - 2 * (m // 3)
        return ((z + SIDE - dz) % SIDE) * 2 + (core + n % 2) % 2

    def fill(dst, own, anc, p):
        dst[0:slot] = own[:, lanes(p)]
        for a in range(2):
            dst[(a + 1) * slot:(a + 2) * slot] = anc[p * 2 + a]

    def column(row):
        return jnp.broadcast_to(row, (DH, slot)).T

    def hand_back(terms, own, fb, far, n, p, handles):
        own[p] = terms[0:slot]
        for a in range(2):
            fb[p * 2 + a] = terms[(a + 1) * slot:(a + 2) * slot].astype(BF)

        @pl.when(n > 0)
        def _():
            start(handles[0].n + n - 1, fb.at[pl.ds(p * 2, 2)], far.at[pl.ds(head * 2, 2)], seg, p)

    def arrived(handles, n):
        @pl.when(n > 0)
        def _():
            Handle(handles[0].n + n - 1, two_blocks).wait_recv()

    def pass_one(n, handles):
        p = giver(n)
        fill(kc, kown, anc_k, p)
        for j in range(group):
            place = lanes(p * group + j)
            span = slice(j * slot, (j + 1) * slot)
            s = lax.dot_general(kc[...], qv[:, place], nt, preferred_element_type=F32) + bias[...]
            top = jnp.max(s, axis=0, keepdims=True)
            e = jnp.exp2((s - top) * exp_scale)
            inv = 1.0 / jnp.sum(e, axis=0, keepdims=True)
            ec[n, :, span] = e.astype(BF)
            invs[n, :, span] = inv
            g = (gv[:, place] * live[...]).astype(F32)
            gs[span] = (g * column(inv)).astype(BF)
        terms = jnp.dot(ec[n], gs[...], preferred_element_type=F32)
        hand_back(terms, own_v, fb_v, far_v, n, p, handles)

    def pass_two(n, handles):
        p = giver(n)
        fill(kc, kown, anc_k, p)
        fill(vc, vown, anc_v, p)
        kt[...] = kc[...].T
        for j in range(group):
            place = lanes(p * group + j)
            span = slice(j * slot, (j + 1) * slot)
            g = gv[:, place] * live[...]
            wg = lax.dot_general(vc[...], g, nt, preferred_element_type=F32)
            e = ec[n, :, span].astype(F32)
            inv = invs[n, :, span]
            delta = jnp.sum(e * wg, axis=0, keepdims=True) * inv
            dcat[:, span] = (e * (wg - delta)).astype(BF)
            qs[span] = (qv[:, place].astype(F32) * column(inv)).astype(BF)
        terms = jnp.dot(dcat[...], qs[...], preferred_element_type=F32) * scale
        hand_back(terms, own_k, fb_k, far_k, n, p, handles)
        dqt = jnp.dot(kt[...], dcat[...], preferred_element_type=F32) * (invs[n] * scale)
        for j in range(group):
            dqv[:, lanes(p * group + j)] = dqt[:, j * slot:(j + 1) * slot].T.astype(BF)
        wide = pl.ds(pl.multiple_of(p * (group * DH), DH), group * DH)
        pltpu.make_async_copy(dqv.at[:, wide], dq_ref.at[0, :, wide], out_sem.at[n]).start()

    links = 2 * NHEAD

    def sums(far, accs, tt):
        def add(n, acc):
            acc = far[tab[T_ORDER + n]].astype(F32) + acc * tab[T_CONT + n].astype(F32)
            accs[n] = acc.astype(BF)
            return acc

        lax.fori_loop(0, links, add, jnp.zeros((slot, DH), F32))
        accs[links] = jnp.zeros((slot, DH), BF)

        def spread(j, carry):
            tt[j] = accs[tab[T_LAST + j]]
            return carry

        lax.fori_loop(0, NCOL * PUB, spread, 0)

    def plus(*terms):
        total = terms[0].astype(F32)
        for term in terms[1:]:
            total = total + term.astype(F32)
        return total.astype(BF)

    class Scatter:
        def __init__(self, far, back, fb, accs, tt, half, full, fin):
            self.fb = fb
            self.far, self.back, self.accs, self.tt = far, back, accs, tt
            self.half, self.full, self.fin = half, full, fin

        def block(self, r, axis, da, db):
            return self.tt.at[at(axis, da, db) * PUB + r]

        def send_far(self, r, axis, other, slot_no):
            ref = self.block(r, axis, 2, other)
            out = []
            for part, step in ((0, 1), (1, 3)):
                out.append(push(ref.at[pl.ds(part * mid, mid)], self.half.at[(r * 4 + slot_no) * 2 + part],
                                along(axis, step), head, half_block))
            return out

        def send_near(self, r, axis, other, slot_no, pair):
            out = []
            for part, step in ((0, 1), (1, 3)):
                pair[part].wait_recv()
                ref = self.block(r, axis, step, other)
                span = pl.ds(part * mid, mid)
                ref[span] = plus(ref[span], self.half[(r * 4 + slot_no) * 2 + part])
                out.append(push(ref, self.full.at[(r * 4 + slot_no) * 2 + part], along(axis, step), head, one_block))
            return out

        def total(self, r, axis, other, slot_no, pair):
            for copy in pair:
                copy.wait_recv()
            ref = self.block(r, axis, 0, other)
            n = (r * 4 + slot_no) * 2
            return ref, plus(ref[...], self.full[n], self.full[n + 1])

        def steps(self):
            for copy in self.back:
                copy.wait_recv()
            settle(self.tt)
            for a in range(2):
                self.far[head * 2 + a] = self.fb[head * 2 + a]
            sums(self.far, self.accs, self.tt)
            a, b = {}, {}
            for r in range(PUB):
                for other in (2, 1, 3, 0):
                    a[r, other] = self.send_far(r, 1 - r, other, other)
            yield
            for other in (2, 1, 3, 0):
                for r in range(PUB):
                    b[r, other] = self.send_near(r, 1 - r, other, other, a[r, other])
            yield
            for step in (2, 1, 3):
                for r in range(PUB):
                    ref, value = self.total(r, 1 - r, step, step, b[r, step])
                    ref[...] = value
                    a[r, 4, step] = push(ref, self.full.at[self.place(r, step)], along(r, step), head, one_block)
            yield
            for r in range(PUB):
                ref, value = self.total(r, 1 - r, 0, 0, b[r, 0])
                ref[...] = value
            yield
            for r in range(PUB):
                for step in (1, 3, 2):
                    a[r, 4, step].wait_recv()
                self.fin[r] = plus(self.block(r, r, 0, 0)[...], *[self.full[self.place(r, step)] for step in (1, 3, 2)])

        def place(self, r, step):
            return 4 * PUB * 2 + r * 3 + step - 1

    def give(fin, rb, ret):
        out = []
        settle(rb)
        for step in PEERS:
            p = peer(step)
            rb[p] = fin[tab[T_RANK + p]]
            out.append(push(rb.at[p], ret.at[head], seg, p, one_block))
        ret[head] = fin[tab[T_RANK + head]]
        return out

    loads[0].wait()
    for copy in first_k:
        copy.wait_recv()
    first_v = offer(v_ref, all_v)
    gather_k = Gather(sh_k, all_k, kown).steps()
    gather_v = Gather(sh_v, all_v, vown).steps()
    for _ in range(4):
        run(gather_k)
    loads[1].wait()
    for copy in first_v:
        copy.wait_recv()
    run(gather_v)
    run(gather_k)
    run(gather_v)
    run(gather_k)
    got_k = select(sh_k, sel_k, anc_k)
    loads[2].wait()
    loads[3].wait()
    back_v = reserve(len(PEERS), two_blocks)
    back_k = reserve(len(PEERS), two_blocks)
    got_v = []

    def first_loop(n, carry):
        arrived(got_k, n)
        pass_one(n, back_v)
        for i in range(4):
            @pl.when(n == i)
            def _():
                run(gather_v)
                if i == 3:
                    got_v.extend(select(sh_v, sel_v, anc_v))
        return carry

    lax.fori_loop(0, NHEAD, first_loop, 0)
    scatter_k = Scatter(far_k, back_k, fb_k, accs_k, sh_k, half_k, full_k, fin_k).steps()
    scatter_v = Scatter(far_v, back_v, fb_v, accs_v, sh_v, half_v, full_v, fin_v).steps()

    def second_loop(n, carry):
        arrived(got_v, n)
        pass_two(n, back_k)
        for i in range(2):
            @pl.when(n == i + 6)
            def _():
                run(scatter_v)
        return carry

    lax.fori_loop(0, NHEAD, second_loop, 0)
    run(scatter_v)
    run(scatter_k)
    run(scatter_v)
    run(scatter_k)
    run(scatter_v)
    give_v = give(fin_v, sel_v, ret_v)
    run(scatter_k)
    run(scatter_k)
    run(scatter_k)
    give_k = give(fin_k, sel_k, ret_k)
    inner = tab[T_OWN + 3] > 0

    for copies, own, ret, out in ((give_v, own_v, ret_v, dv_ref), (give_k, own_k, ret_k, dk_ref)):
        for copy in copies:
            copy.wait_recv()
        for p in range(NHEAD):
            out[0, :, p * DH:(p + 1) * DH] = (
                own[p] + jnp.where(inner, ret[p].astype(F32), 0.0)).astype(BF)

    for copy in sent:
        copy.wait_send()
    for n in range(NHEAD):
        wide = pl.ds(0, group * DH)
        pltpu.make_async_copy(dqv.at[:, wide], dq_ref.at[0, :, wide], out_sem.at[n]).wait()


def body(queries, key_states, values, grad_out, owners, parents, depths, lengths):
    tab = tables_of(owners, parents, depths, lengths)
    _, slot, width = queries.shape
    kv_width = key_states.shape[2]
    group = width // kv_width
    any_space = pl.BlockSpec(memory_space=pl.ANY)
    vmem = pl.BlockSpec(memory_space=pltpu.VMEM)

    def blocks(n, rows=slot, dtype=BF):
        return [pltpu.VMEM((n, rows, DH), dtype)] * 2

    scratch = (
        [pltpu.VMEM((slot, width), BF)] * 2
        + [pltpu.VMEM((slot, kv_width), BF)] * 2
        + blocks(NHEAD)
        + blocks(NCOL * PUB)
        + blocks(2 * NHEAD)
        + blocks(2 * NHEAD)
        + blocks(NHEAD, dtype=F32)
        + blocks(2 * NHEAD)
        + blocks(2 * NHEAD)
        + blocks(2 * NHEAD + 1)
        + blocks(PUB * 4 * 2, slot // 2)
        + blocks(PUB * (4 * 2 + 3))
        + blocks(PUB)
        + blocks(NHEAD)
        + [
            pltpu.VMEM((slot, width), BF),
            pltpu.VMEM((3 * slot, slot), F32),
            pltpu.VMEM((slot, DH), BF),
            pltpu.VMEM((3 * slot, DH), BF),
            pltpu.VMEM((3 * slot, DH), BF),
            pltpu.VMEM((DH, 3 * slot), BF),
            pltpu.VMEM((NHEAD, 3 * slot, group * slot), BF),
            pltpu.VMEM((3 * slot, group * slot), BF),
            pltpu.VMEM((group * slot, DH), BF),
            pltpu.VMEM((group * slot, DH), BF),
            pltpu.VMEM((NHEAD, 1, group * slot), F32),
            pltpu.SemaphoreType.DMA((216,)),
            pltpu.SemaphoreType.DMA((216,)),
            pltpu.SemaphoreType.DMA((4,)),
            pltpu.SemaphoreType.DMA((NHEAD,)),
        ]
    )
    return pl.pallas_call(
        kernel,
        out_shape=(
            jax.ShapeDtypeStruct(queries.shape, BF),
            jax.ShapeDtypeStruct(key_states.shape, BF),
            jax.ShapeDtypeStruct(values.shape, BF),
        ),
        in_specs=[pl.BlockSpec(memory_space=pltpu.SMEM)] + [any_space] * 4,
        out_specs=(any_space, vmem, vmem),
        scratch_shapes=scratch,
        compiler_params=pltpu.CompilerParams(
            collective_id=0, has_side_effects=True, vmem_limit_bytes=63 * 2**20),
        cost_estimate=pl.CostEstimate(
            flops=10 * QH_FLOPS * slot, bytes_accessed=10 * 2**20, transcendentals=slot * 3 * slot * width // DH),
    )(tab, queries, key_states, values, grad_out)


QH_FLOPS = 40 * 768 * 128


def solution(mesh):
    placed = (P(("seg", "head"), None, None),) * 4 + (P(),) * 4
    return jax.shard_map(
        body,
        mesh=mesh,
        in_specs=placed,
        out_specs=(P(("seg", "head"), None, None),) * 3,
        check_vma=False,
    )
```

profile of v0, /device:TPU:1, one launch (start us, length us, event | category | flops | bytes accessed | tf_op | source)
XLA Modules:
  0.0 121.5 jit_solution(3341129217803847325)
XLA Ops:
  0.6 2.1 %shard_map.103.tab = s32[96]{0:T(128)} custom-call(s32[128]{0:T(128)} %owners.1, s32[128]{0:T(128)} %parents.1, s32[128]{0:T(128)} %depths.1, s32[128]{0:T(128)} %lengths.1), custom_call_target="tpu_custom_call" | custom-call | tf_op jit(solution)/shard_map/pallas_call | solution.py:93
  2.7 113.7 %shard_map.104 = (bf16[1,256,5120]{2,1,0:T(8,128)(2,1)}, bf16[1,256,1024]{2,1,0:T(8,128)(2,1)}, bf16[1,256,1024]{2,1,0:T(8,128)(2,1)}) custom-call(s32[96]{0:T(128)} %shard_map.103.tab, bf16[1,256,5120]{2,1,0:T(8,128)(2,1)} %q_ref.1, bf16[1,256,1024]{2,1,0:T(8,128)(2,1)} %k_ref.1, bf16[1,256,1024]{2,1,0:T(8,128)(2,1)} %v_ref.1, bf16[1,256,5120]{2,1,0:T(8,128)(2,1)} %g_ref.1), custom_call_target="tpu_custom_call" | custom-call | flops 10066329600 | bytes 10485760 | tf_op jit(solution)/shard_map/pallas_call | solution.py:568
  116.4 0.0 copy-start.1
  116.4 0.0 copy-start
  116.4 3.5 %copy.14 = bf16[1,256,5120]{2,1,0:T(8,128)(2,1)} copy(bf16[1,256,5120]{2,1,0:T(8,128)(2,1)} %get-tuple-element.6) | data formatting | bytes 5242880
  119.9 0.0 copy-done.1
  119.9 0.8 copy.15
  120.7 0.0 copy-done
  120.7 0.8 copy.16
Async XLA Ops:
  116.4 3.5 %copy-start.1 = (bf16[1,256,1024]{2,1,0:T(8,128)(2,1)S(1)}, bf16[1,256,1024]{2,1,0:T(8,128)(2,1)}, u32[]{:S(2)}) copy-start(bf16[1,256,1024]{2,1,0:T(8,128)(2,1)} %get-tuple-element.7) | copy-start | bytes 1572868
  116.4 4.3 %copy-start = (bf16[1,256,1024]{2,1,0:T(8,128)(2,1)S(1)}, bf16[1,256,1024]{2,1,0:T(8,128)(2,1)}, u32[]{:S(2)}) copy-start(bf16[1,256,1024]{2,1,0:T(8,128)(2,1)} %get-tuple-element.8) | copy-start | bytes 1572868
where the time goes:
time: 122 us
  Pallas kernels  116 us (95%)
  local copies, waits for them, and re-layouts  5.08 us (4%)
    pallas_call x1, Pallas kernels, body(): pl.pallas_call(kernel, out_shape=(jax.ShapeDtypeStruct(queries.shape, BF)...  114 us
    unnamed x7, local copies, waits for them, and re-layouts  5.08 us

commit v1 on v0

--- a/solution.py
+++ b/solution.py
@@ -234,10 +234,13 @@
             a, b, relays = {}, {}, []
             for r in range(PUB):
                 ref = self.block(r, 0, 0)
-                a[r] = [push(ref, ref, along(r, step), head, one_block, self.sh) for step in (1, 3, 2)]
+                a[r] = [push(ref, ref, along(r, step), head, one_block, self.sh) for step in (1, 3)]
             yield
             for r in range(PUB):
                 b[r, 0] = self.spread(r, 1 - r, 0, 0)
+            for r in range(PUB):
+                ref = self.block(r, 0, 0)
+                a[r].append(push(ref, ref, along(r, 2), head, one_block, self.sh))
             for r in range(PUB):
                 for came, da in ((0, 3), (1, 1)):
                     a[r][came].wait_recv()
@@ -355,14 +358,14 @@
             accs[n] = acc.astype(BF)
             return acc
 
-        lax.fori_loop(0, links, add, jnp.zeros((slot, DH), F32))
+        lax.fori_loop(0, links, add, jnp.zeros((slot, DH), F32), unroll=4)
         accs[links] = jnp.zeros((slot, DH), BF)
 
         def spread(j, carry):
             tt[j] = accs[tab[T_LAST + j]]
             return carry
 
-        lax.fori_loop(0, NCOL * PUB, spread, 0)
+        lax.fori_loop(0, NCOL * PUB, spread, 0, unroll=4)
 
     def plus(*terms):
         total = terms[0].astype(F32)
@@ -519,6 +522,15 @@
     for n in range(NHEAD):
         wide = pl.ds(0, group * DH)
         pltpu.make_async_copy(dqv.at[:, wide], dq_ref.at[0, :, wide], out_sem.at[n]).wait()
+
+
+PARTS = 4
+
+
+def place_kernel(dq, dk, dv, dq_out, dk_out, dv_out):
+    dq_out[...] = dq[...]
+    dk_out[...] = dk[...]
+    dv_out[...] = dv[...]
 
 
 def body(queries, key_states, values, grad_out, owners, parents, depths, lengths):
@@ -565,7 +577,7 @@
             pltpu.SemaphoreType.DMA((NHEAD,)),
         ]
     )
-    return pl.pallas_call(
+    grads = pl.pallas_call(
         kernel,
         out_shape=(
             jax.ShapeDtypeStruct(queries.shape, BF),
@@ -580,6 +592,14 @@
         cost_estimate=pl.CostEstimate(
             flops=10 * QH_FLOPS * slot, bytes_accessed=10 * 2**20, transcendentals=slot * 3 * slot * width // DH),
     )(tab, queries, key_states, values, grad_out)
+    blocks_of = [pl.BlockSpec((1, slot // PARTS, grad.shape[2]), lambda i: (0, i, 0)) for grad in grads]
+    return pl.pallas_call(
+        place_kernel,
+        grid=(PARTS,),
+        out_shape=tuple(jax.ShapeDtypeStruct(grad.shape, BF) for grad in grads),
+        in_specs=blocks_of,
+        out_specs=tuple(blocks_of),
+    )(*grads)
 
 
 QH_FLOPS = 40 * 768 * 128

time: 122 us -> 120 us (0.984)
  local copies, waits for them, and re-layouts: 5.08 us -> 0 us
  Pallas kernels: 116 us -> 119 us
    unnamed x7 -> x0, local copies, waits for them, and re-layouts: 5.08 us -> none
    pallas_call x0 -> x1, Pallas kernels: none -> 4.4 us  [body(): pl.pallas_call(place_kernel, grid=(PARTS,), out_shape=tuple((jax.ShapeDty...]
    pallas_call x1, Pallas kernels: 114 us -> 112 us  [body(): pl.pallas_call(kernel, out_shape=(jax.ShapeDtypeStruct(queries.shape, BF)...]
where the time goes in v1:
time: 120 us
  Pallas kernels  119 us (99%)
    pallas_call x1, Pallas kernels, body(): pl.pallas_call(kernel, out_shape=(jax.ShapeDtypeStruct(queries.shape, BF)...  112 us
    pallas_call x1, Pallas kernels, body(): pl.pallas_call(place_kernel, grid=(PARTS,), out_shape=tuple((jax.ShapeDty...  4.4 us

profile of v1, /device:TPU:1, one launch (start us, length us, event | category | flops | bytes accessed | tf_op | source)
XLA Modules:
  0.0 119.6 jit_solution(13535787236858331290)
XLA Ops:
  0.6 2.1 %shard_map.103.tab = s32[96]{0:T(128)} custom-call(s32[128]{0:T(128)} %owners.1, s32[128]{0:T(128)} %parents.1, s32[128]{0:T(128)} %depths.1, s32[128]{0:T(128)} %lengths.1), custom_call_target="tpu_custom_call" | custom-call | tf_op jit(solution)/shard_map/pallas_call | solution.py:93
  2.7 112.4 %shard_map.104 = (bf16[1,256,5120]{2,1,0:T(8,128)(2,1)}, bf16[1,256,1024]{2,1,0:T(8,128)(2,1)}, bf16[1,256,1024]{2,1,0:T(8,128)(2,1)}) custom-call(s32[96]{0:T(128)} %shard_map.103.tab, bf16[1,256,5120]{2,1,0:T(8,128)(2,1)} %q_ref.1, bf16[1,256,1024]{2,1,0:T(8,128)(2,1)} %k_ref.1, bf16[1,256,1024]{2,1,0:T(8,128)(2,1)} %v_ref.1, bf16[1,256,5120]{2,1,0:T(8,128)(2,1)} %g_ref.1), custom_call_target="tpu_custom_call" | custom-call | flops 10066329600 | bytes 10485760 | tf_op jit(solution)/shard_map/pallas_call | solution.py:580
  115.2 4.4 %shard_map.105 = (bf16[1,256,5120]{2,1,0:T(8,128)(2,1)}, bf16[1,256,1024]{2,1,0:T(8,128)(2,1)}, bf16[1,256,1024]{2,1,0:T(8,128)(2,1)}) custom-call(bf16[1,256,5120]{2,1,0:T(8,128)(2,1)} %get-tuple-element.6.dq, bf16[1,256,1024]{2,1,0:T(8,128)(2,1)} %get-tuple-element.7.dk, bf16[1,256,1024]{2,1,0:T(8,128)(2,1)} %get-tuple-element.8.dv), custom_call_target="tpu_custom_call" | custom-call | tf_op jit(solution)/shard_map/pallas_call | solution.py:596
